TPU v7x, 32 devices: a whole 2x2x4 slice. The times are simulated.
32 devices in a mesh: cuts: 2 (over x), tile: 16 (over z, y, core).
Axes of the slice: x: 2, y: 2, z: 4, core: 2. Of those that a mesh axis runs over, the one named last changes fastest.
Arguments:
- trans_real: float32 [2, 4096, 256], P('cuts', 'tile'), may hold values from 0.6 to 1.4
- trans_imag: float32 [2, 4096, 256], P('cuts', 'tile'), may hold values from -1.5 to 1.5
- probe_real: bfloat16 [128, 128], replicated, may hold values from -6 to 6
- probe_imag: bfloat16 [128, 128], replicated, may hold values from -6 to 6
- offsets: int32 [2, 512], P(None, 'tile'), may hold values from 0 to 128
- pattern_index: int32 [512], P('tile'), may hold values from 0 to 511, as said below
- measured: bfloat16 [512, 128, 128], P('tile'), may hold values from 0.19921875 to 3
Outputs:
- object_grad: float32 [2, 2, 4096, 256], P(None, 'cuts', 'tile')
Inputs may be any that keep to these rules, and one draw needn't show every extreme that they name: `pattern_index`: each row of measured is named by exactly one position; row r is stored with tile r // 32. Of the positions of one tile at most 2 have patterns stored with any one tile, and every tile has exactly 2 with some tile.
All inputs are finite; a program needn't handle non-finite values.
Results may differ from a plain program's by a relative error of at most 0.015.
The roundings to bfloat16 on the way count: a program that leaves them out, or rounds other values in their place, can miss the bound.
Values may be sent and summed in bfloat16 or wider, within the bound.
A program may use at most 64 MiB of HBM per device.

v0:
```python
import math

import jax
import jax.numpy as jnp
from jax import lax
from jax.sharding import PartitionSpec as P

MICRO = 8


fresnel_strength = 9.0
softening = 0.01


def tables(extent):
    indices = jnp.arange(extent, dtype=jnp.int32)
    products = indices[:, None] * indices[None, :] % extent
    angles = products.astype(jnp.float32) * (2.0 * math.pi / extent)
    cosine = jnp.cos(angles)
    sines = jnp.sin(angles)
    frequency = (
        jnp.where(indices < (extent + 1) // 2, indices, indices - extent).astype(jnp.float32)
        / extent
    )
    phases = -fresnel_strength * frequency * frequency
    kernel_real = jnp.cos(phases)
    kernel_imag = jnp.sin(phases)
    scaled_real = cosine * kernel_real[None, :] - sines * kernel_imag[None, :]
    scaled_imag = cosine * kernel_imag[None, :] + sines * kernel_real[None, :]
    highest = lax.Precision.HIGHEST
    prop_real = (
        jnp.dot(scaled_real, cosine, precision=highest)
        + jnp.dot(scaled_imag, sines, precision=highest)
    ) / extent
    prop_imag = (
        jnp.dot(scaled_imag, cosine, precision=highest)
        - jnp.dot(scaled_real, sines, precision=highest)
    ) / extent
    norming = 1.0 / math.sqrt(extent)
    return (
        prop_real.astype(jnp.bfloat16),
        prop_imag.astype(jnp.bfloat16),
        (cosine * norming).astype(jnp.bfloat16),
        (-sines * norming).astype(jnp.bfloat16),
    )


def left_product(matrix, field):
    return jnp.einsum("ab,nbc->nac", matrix, field, preferred_element_type=jnp.float32)


def right_product(field, matrix):
    return jnp.einsum("nab,bc->nac", field, matrix, preferred_element_type=jnp.float32)


def apply_both(mat_real, mat_imag, field_real, field_imag):
    mid_real = (left_product(mat_real, field_real) - left_product(mat_imag, field_imag)).astype(
        jnp.bfloat16
    )
    mid_imag = (left_product(mat_real, field_imag) + left_product(mat_imag, field_real)).astype(
        jnp.bfloat16
    )
    end_real = right_product(mid_real, mat_real) - right_product(mid_imag, mat_imag)
    end_imag = right_product(mid_real, mat_imag) + right_product(mid_imag, mat_real)
    return (end_real, end_imag)


def windows(patch_grid, offset_sel, extent):

    def cut_one(row_at, col_at):
        return lax.dynamic_slice(patch_grid, (row_at, col_at), (extent, extent))

    return jax.vmap(cut_one)(offset_sel[0], offset_sel[1])


def accumulate(patch_grid, contrib, offset_sel, extent):

    def add_one(item, acc):
        row_at = offset_sel[0, item]
        col_at = offset_sel[1, item]
        current = lax.dynamic_slice(acc, (row_at, col_at), (extent, extent))
        return lax.dynamic_update_slice(acc, current + contrib[item], (row_at, col_at))

    return lax.fori_loop(0, contrib.shape[0], add_one, patch_grid)


def forward_slice(win_real, win_imag, wave_real, wave_imag, prop_real, prop_imag):
    field_real = (
        win_real * wave_real.astype(jnp.float32) - win_imag * wave_imag.astype(jnp.float32)
    ).astype(jnp.bfloat16)
    field_imag = (
        win_real * wave_imag.astype(jnp.float32) + win_imag * wave_real.astype(jnp.float32)
    ).astype(jnp.bfloat16)
    out_real, out_imag = apply_both(prop_real, prop_imag, field_real, field_imag)
    return jnp.stack([out_real.astype(jnp.bfloat16), out_imag.astype(jnp.bfloat16)])


def modulus(exit_real, exit_imag, amplitude, four_real, four_imag):
    far_real, far_imag = apply_both(four_real, four_imag, exit_real, exit_imag)
    amp = jnp.sqrt(far_real * far_real + far_imag * far_imag + softening)
    ratio = (amp - amplitude.astype(jnp.float32)) / amp
    resid_real = (ratio * far_real).astype(jnp.bfloat16)
    resid_imag = (ratio * far_imag).astype(jnp.bfloat16)
    back_real, back_imag = apply_both(four_real, -four_imag, resid_real, resid_imag)
    return (back_real.astype(jnp.bfloat16), back_imag.astype(jnp.bfloat16))


def backward_slice(
    win_real, win_imag, grad_real, grad_imag, wave_real, wave_imag, prop_real, prop_imag
):
    back_real, back_imag = apply_both(prop_real, -prop_imag, grad_real, grad_imag)
    psi_real = wave_real.astype(jnp.float32)
    psi_imag = wave_imag.astype(jnp.float32)
    contrib_real = back_real * psi_real + back_imag * psi_imag
    contrib_imag = back_imag * psi_real - back_real * psi_imag
    out_real = (back_real * win_real + back_imag * win_imag).astype(jnp.bfloat16)
    out_imag = (back_imag * win_real - back_real * win_imag).astype(jnp.bfloat16)
    return (contrib_real, contrib_imag, jnp.stack([out_real, out_imag]))


def fetch_patterns(pattern_index, measured, tile_count, capacity):
    positions = pattern_index.shape[0]
    owners = pattern_index // positions
    slots = pattern_index % positions
    ordinal = jnp.arange(positions, dtype=jnp.int32)
    shared = (owners[:, None] == owners[None, :]) & (ordinal[:, None] < ordinal[None, :])
    ranks = jnp.sum(shared.astype(jnp.int32), axis=0)
    target = owners * capacity + ranks
    request = jnp.zeros((tile_count * capacity,), jnp.int32).at[target].set(slots)
    requested = lax.all_to_all(request, "tile", split_axis=0, concat_axis=0, tiled=True)
    rows_out = jnp.take(measured, requested, axis=0)
    answered = lax.all_to_all(rows_out, "tile", split_axis=0, concat_axis=0, tiled=True)
    return jnp.take(answered, target, axis=0)


def local(trans_real, trans_imag, probe_real, probe_imag, offsets, pattern_index, measured):
    extent = probe_real.shape[-1]
    positions = pattern_index.shape[0]
    tile_count = lax.axis_size("tile")
    sections = lax.axis_size("cuts")
    section_no = lax.axis_index("cuts")
    capacity = (positions + tile_count - 1) // tile_count
    micro_count = MICRO
    per_batch = positions // micro_count
    prop_real, prop_imag, four_real, four_imag = tables(extent)
    amplitude = fetch_patterns(pattern_index, measured, tile_count, capacity)
    whole_real, whole_imag = (
        lax.all_gather(trans_real, "cuts", axis=0, tiled=True),
        lax.all_gather(trans_imag, "cuts", axis=0, tiled=True),
    )
    my_share = micro_count // sections
    mine_count = my_share * per_batch
    offset_mine = lax.dynamic_index_in_dim(
        offsets.reshape(2, my_share, sections, per_batch), section_no, 2, keepdims=False
    ).reshape(2, mine_count)
    amp_mine = lax.dynamic_index_in_dim(
        amplitude.reshape(my_share, sections, per_batch, extent, extent),
        section_no,
        1,
        keepdims=False,
    ).reshape(mine_count, extent, extent)
    probe_wave = jnp.stack(
        [
            jnp.broadcast_to(probe_real, (mine_count, extent, extent)),
            jnp.broadcast_to(probe_imag, (mine_count, extent, extent)),
        ]
    )

    def descend(wave_in, slab):
        slab_real, slab_imag = slab
        win_real = windows(slab_real, offset_mine, extent)
        win_imag = windows(slab_imag, offset_mine, extent)
        out_wave = forward_slice(win_real, win_imag, wave_in[0], wave_in[1], prop_real, prop_imag)
        return (out_wave, wave_in)

    exit_wave, stored = lax.scan(descend, probe_wave, (whole_real, whole_imag))
    seed_real, seed_imag = modulus(exit_wave[0], exit_wave[1], amp_mine, four_real, four_imag)
    grid_zero = jnp.zeros(whole_real.shape[1:], jnp.float32)

    def ascend(wave_in, slab):
        slab_real, slab_imag, psi_wave = slab
        win_real = windows(slab_real, offset_mine, extent)
        win_imag = windows(slab_imag, offset_mine, extent)
        contrib_real, contrib_imag, out_wave = backward_slice(
            win_real,
            win_imag,
            wave_in[0],
            wave_in[1],
            psi_wave[0],
            psi_wave[1],
            prop_real,
            prop_imag,
        )
        grad_real = accumulate(grid_zero, contrib_real, offset_mine, extent)
        grad_imag = accumulate(grid_zero, contrib_imag, offset_mine, extent)
        return (out_wave, (grad_real, grad_imag))

    _, slab_grads = lax.scan(
        ascend, jnp.stack([seed_real, seed_imag]), (whole_real, whole_imag, stored), reverse=True
    )
    part_real, part_imag = (
        lax.psum_scatter(slab_grads[0], "cuts", scatter_dimension=0, tiled=True),
        lax.psum_scatter(slab_grads[1], "cuts", scatter_dimension=0, tiled=True),
    )
    return jnp.stack([part_real, part_imag])


def solution(mesh):
    return jax.shard_map(
        local,
        mesh=mesh,
        in_specs=(
            P("cuts", "tile", None),
            P("cuts", "tile", None),
            P(),
            P(),
            P(None, "tile"),
            P("tile"),
            P("tile", None, None),
        ),
        out_specs=P(None, "cuts", "tile", None),
        check_vma=False,
    )
```

profile of v0, /device:TPU:0, one launch (start us, length us, event | category | flops | bytes accessed | tf_op | source)
XLA Modules:
  0.0 908.5 jit_solution(15004787042793693076)
XLA Ops:
  8.8 7.4 all-to-all-start
  17.2 12.3 %all_gather.6 = f32[2,256,256]{2,1,0:T(8,128)} all-gather(f32[1,256,256]{2,1,0:T(8,128)} %param.17), channel_id=1, replica_groups=mesh['cuts'=2,'tile'=16] {'cuts'}, dimensions={0}, use_global_device_ids=true | all-gather | bytes 786432 | tf_op jit(solution)/shard_map/all_gather | solution.py:148
  30.4 8.8 all_gather.7
  40.5 168.3 %while.92 = (s32[]{:T(128)}, bf16[2,16,128,128]{3,2,1,0:T(8,128)(2,1)S(1)}, bf16[2,2,16,128,128]{4,3,2,1,0:T(8,128)(2,1)}, f32[2,256,256]{2,1,0:T(8,128)}, s32[2...) while((s32[]{:T(128)}, ...), condition=%wide.region_1.2_spmd, body=%wide.region_0.1_spmd.sunk | while | flops 542113920 | bytes 30934012 | solution.py:176
  43.5 45.0 %while.98 = (s32[]{:T(128)}, f32[256,256]{1,0:T(8,128)}, s32[16,2]{0,1:T(2,128)S(1)}, f32[16,128,128]{2,1,0:T(8,128)S(1)}, s32[]{:T(128)}) while((s32[]{:T(128)}, f32[256,256]{1,0:T(8,128)}, s32[16,2]{0,1:T(2,128)S(1)}, f32[16,128,128]{2,1,0:T(8,128)S(1)}, s32[]{:T(128)}) %tuple.230), condition=%wide.while_cond, body=%wide.while_body.sunk | while | flops 2 | bytes 131189 | solution.py:71
  52.5 2.2 bitcast_dynamic-update-slice_fusion.17
  89.6 30.6 %while.99 = (s32[]{:T(128)}, f32[256,256]{1,0:T(8,128)S(1)}, s32[16,2]{0,1:T(2,128)S(1)}, f32[16,128,128]{2,1,0:T(8,128)S(1)}, s32[]{:T(128)}) while((s32[]{:T(128)}, f32[256,256]{1,0:T(8,128)S(1)}, s32[16,2]{0,1:T(2,128)S(1)}, f32[16,128,128]{2,1,0:T(8,128)S(1)}, s32[]{:T(128)}) %tuple.249), condition=%wide.while_cond.1, body=%wide.while_body.1.sunk | while | flops 2 | bytes 131189 | solution.py:71
  127.6 45.0 %while.98 = (s32[]{:T(128)}, f32[256,256]{1,0:T(8,128)}, s32[16,2]{0,1:T(2,128)S(1)}, f32[16,128,128]{2,1,0:T(8,128)S(1)}, s32[]{:T(128)}) while((s32[]{:T(128)}, f32[256,256]{1,0:T(8,128)}, s32[16,2]{0,1:T(2,128)S(1)}, f32[16,128,128]{2,1,0:T(8,128)S(1)}, s32[]{:T(128)}) %tuple.230), condition=%wide.while_cond, body=%wide.while_body.sunk | while | flops 2 | bytes 131189 | solution.py:71
  173.8 30.6 %while.99 = (s32[]{:T(128)}, f32[256,256]{1,0:T(8,128)S(1)}, s32[16,2]{0,1:T(2,128)S(1)}, f32[16,128,128]{2,1,0:T(8,128)S(1)}, s32[]{:T(128)}) while((s32[]{:T(128)}, f32[256,256]{1,0:T(8,128)S(1)}, s32[16,2]{0,1:T(2,128)S(1)}, f32[16,128,128]{2,1,0:T(8,128)S(1)}, s32[]{:T(128)}) %tuple.249), condition=%wide.while_cond.1, body=%wide.while_body.1.sunk | while | flops 2 | bytes 131189 | solution.py:71
  212.7 5.7 all-to-all-start.1
  223.6 17.7 %all-to-all-done.1 = bf16[32,128,128]{2,1,0:T(8,128)(2,1)} async-done(((bf16[32,128,128]{2,1,0:T(8,128)(2,1)}), bf16[32,128,128]{2,1,0:T(8,128)(2,1)}, u32[]{:S(2)}, u32[]{:S(2)}) %all-to-all-start.1) | async-done | bytes 1048608 | tf_op jit(solution)/shard_map/all_to_all | solution.py:132
  253.0 606.3 %while.97 = (s32[]{:T(128)}, bf16[2,16,128,128]{3,2,1,0:T(8,128)(2,1)}, f32[2,256,256]{2,1,0:T(8,128)}, f32[2,256,256]{2,1,0:T(8,128)}, bf16[128,128]{1,0:T(8,12...) while((s32[]{:T(128)}, ...), condition=%wide.region_9.11_spmd, body=%wide.region_4.10_spmd.sunk | while | flops 543195264 | bytes 40503928 | solution.py:198
  258.6 31.3 %while.100 = (s32[]{:T(128)}, f32[256,256]{1,0:T(8,128)S(1)}, s32[16,2]{0,1:T(2,128)S(1)}, f32[16,128,128]{2,1,0:T(8,128)S(1)}, s32[]{:T(128)}) while((s32[]{:T(128)}, f32[256,256]{1,0:T(8,128)S(1)}, s32[16,2]{0,1:T(2,128)S(1)}, f32[16,128,128]{2,1,0:T(8,128)S(1)}, s32[]{:T(128)}) %tuple.218), condition=%wide.while_cond.3, body=%wide.while_body.3.sunk | while | flops 2 | bytes 131189 | solution.py:71
  292.2 42.0 %while.101 = (s32[]{:T(128)}, f32[256,256]{1,0:T(8,128)S(1)}, s32[16,2]{0,1:T(2,128)S(1)}, f32[16,128,128]{2,1,0:T(8,128)}, s32[]{:T(128)}) while((s32[]{:T(128)}, f32[256,256]{1,0:T(8,128)S(1)}, s32[16,2]{0,1:T(2,128)S(1)}, f32[16,128,128]{2,1,0:T(8,128)}, s32[]{:T(128)}) %tuple.250), condition=%wide.while_cond.2, body=%wide.while_body.2.sunk | while | flops 2 | bytes 132205 | solution.py:71
  335.4 3.7 fusion.340
  340.2 117.7 %while.102 = (s32[]{:T(128)}, f32[256,256]{1,0:T(8,128)S(1)}, s32[2,16]{1,0:T(2,128)S(1)}, f32[16,128,128]{2,1,0:T(8,128)}, s32[]{:T(128)}, /*index=5*/s32[]{:T(128)}, s32[]{:T(128)}) while((s32[]{:T(128)}, f32[256,256]{1,0:T(8,128)S(1)}, s32[2,16]{1,0:T(2,128)S(1)}, f32[16,128,128]{2,1,0:T(8,128)}, s32[]{:T(128)}, /*index=5*/s32[]{:T(128)}, ...), condition=%wide.region_8.9_spmd, body=%wide.region_7.8_spmd.sunk | while | flops 16392 | bytes 327869 | solution.py:84
  457.9 97.4 %while.103 = (s32[]{:T(128)}, f32[256,256]{1,0:T(8,128)S(1)}, s32[2,16]{1,0:T(2,128)S(1)}, f32[16,128,128]{2,1,0:T(8,128)S(1)}, s32[]{:T(128)}, /*index=5*/s32[]{:T(128)}, s32[]{:T(128)}) while((s32[]{:T(128)}, f32[256,256]{1,0:T(8,128)S(1)}, s32[2,16]{1,0:T(2,128)S(1)}, f32[16,128,128]{2,1,0:T(8,128)S(1)}, s32[]{:T(128)}, ...), condition=%wide.region_6.7_spmd, body=%wide.region_5.6_spmd.sunk | while | flops 16392 | bytes 327869 | solution.py:84
  561.7 31.3 %while.100 = (s32[]{:T(128)}, f32[256,256]{1,0:T(8,128)S(1)}, s32[16,2]{0,1:T(2,128)S(1)}, f32[16,128,128]{2,1,0:T(8,128)S(1)}, s32[]{:T(128)}) while((s32[]{:T(128)}, f32[256,256]{1,0:T(8,128)S(1)}, s32[16,2]{0,1:T(2,128)S(1)}, f32[16,128,128]{2,1,0:T(8,128)S(1)}, s32[]{:T(128)}) %tuple.218), condition=%wide.while_cond.3, body=%wide.while_body.3.sunk | while | flops 2 | bytes 131189 | solution.py:71
  595.4 42.0 %while.101 = (s32[]{:T(128)}, f32[256,256]{1,0:T(8,128)S(1)}, s32[16,2]{0,1:T(2,128)S(1)}, f32[16,128,128]{2,1,0:T(8,128)}, s32[]{:T(128)}) while((s32[]{:T(128)}, f32[256,256]{1,0:T(8,128)S(1)}, s32[16,2]{0,1:T(2,128)S(1)}, f32[16,128,128]{2,1,0:T(8,128)}, s32[]{:T(128)}) %tuple.250), condition=%wide.while_cond.2, body=%wide.while_body.2.sunk | while | flops 2 | bytes 132205 | solution.py:71
  638.6 3.7 fusion.340
  643.3 117.7 %while.102 = (s32[]{:T(128)}, f32[256,256]{1,0:T(8,128)S(1)}, s32[2,16]{1,0:T(2,128)S(1)}, f32[16,128,128]{2,1,0:T(8,128)}, s32[]{:T(128)}, /*index=5*/s32[]{:T(128)}, s32[]{:T(128)}) while((s32[]{:T(128)}, f32[256,256]{1,0:T(8,128)S(1)}, s32[2,16]{1,0:T(2,128)S(1)}, f32[16,128,128]{2,1,0:T(8,128)}, s32[]{:T(128)}, /*index=5*/s32[]{:T(128)}, ...), condition=%wide.region_8.9_spmd, body=%wide.region_7.8_spmd.sunk | while | flops 16392 | bytes 327869 | solution.py:84
  761.0 97.4 %while.103 = (s32[]{:T(128)}, f32[256,256]{1,0:T(8,128)S(1)}, s32[2,16]{1,0:T(2,128)S(1)}, f32[16,128,128]{2,1,0:T(8,128)S(1)}, s32[]{:T(128)}, /*index=5*/s32[]{:T(128)}, s32[]{:T(128)}) while((s32[]{:T(128)}, f32[256,256]{1,0:T(8,128)S(1)}, s32[2,16]{1,0:T(2,128)S(1)}, f32[16,128,128]{2,1,0:T(8,128)S(1)}, s32[]{:T(128)}, ...), condition=%wide.region_6.7_spmd, body=%wide.region_5.6_spmd.sunk | while | flops 16392 | bytes 327869 | solution.py:84
  860.0 22.9 %reduce-scatter.5.cloned.1.call-done = f32[1,256,256]{2,1,0:T(8,128)} async-done(((f32[2,256,256]{2,1,0:T(8,128)}), f32[1,256,256]{2,1,0:T(8,128)}) %reduce-scatter.5.cloned.1.call-update) | async-done | bytes 262160 | tf_op jit(solution)/shard_map/reduce_scatter | solution.py:203
  882.9 16.9 %reduce-scatter.3.cloned.1.call-done = f32[1,256,256]{2,1,0:T(8,128)} async-done(((f32[2,256,256]{2,1,0:T(8,128)}), f32[1,256,256]{2,1,0:T(8,128)}) %reduce-scatter.3.cloned.1.call-update) | async-done | bytes 262160 | tf_op jit(solution)/shard_map/reduce_scatter | solution.py:202
  (724 shorter events, 548.6 us)
Async XLA Ops:
  6.5 204.2 %copy-start = (bf16[32,128,128]{2,1,0:T(8,128)(2,1)S(1)}, bf16[32,128,128]{2,1,0:T(8,128)(2,1)}, u32[]{:S(2)}) copy-start(bf16[32,128,128]{2,1,0:T(8,128)(2,1)} %param.23) | copy-start | bytes 3145732
  6.5 23.8 %copy-start.7 = (f32[1,256,256]{2,1,0:T(8,128)S(1)}, f32[1,256,256]{2,1,0:T(8,128)}, u32[]{:S(2)}) copy-start(f32[1,256,256]{2,1,0:T(8,128)} %param.18) | copy-start | bytes 786436
  6.5 33.6 %copy-start.8 = (bf16[128,128]{1,0:T(8,128)(2,1)S(1)}, bf16[128,128]{1,0:T(8,128)(2,1)}, u32[]{:S(2)}) copy-start(bf16[128,128]{1,0:T(8,128)(2,1)} %param.20) | copy-start | bytes 98308
  8.8 200.7 %all-to-all-start = ((s32[16,2,1]{1,2,0:T(1,128)}), s32[16,2,1]{1,2,0:T(1,128)S(1)}, u32[]{:S(2)}, u32[]{:S(2)}) async-start(s32[16,2,1]{1,2,0:T(1,128)} %bitcast.45), calls=%async_computation | async-start | bytes 16384 | tf_op jit(solution)/shard_map/all_to_all | solution.py:130
  16.7 23.5 %copy-start.9 = (bf16[128,128]{1,0:T(8,128)(2,1)S(1)}, bf16[128,128]{1,0:T(8,128)(2,1)}, u32[]{:S(2)}) copy-start(bf16[128,128]{1,0:T(8,128)(2,1)} %param.19) | copy-start | bytes 98308
  88.6 1.0 copy-start.3
  172.7 1.0 copy-start.3
  212.7 28.7 %all-to-all-start.1 = ((bf16[32,128,128]{2,1,0:T(8,128)(2,1)}), bf16[32,128,128]{2,1,0:T(8,128)(2,1)}, u32[]{:S(2)}, u32[]{:S(2)}) async-start(bf16[32,128,128]{2,1,0:T(8,128)(2,1)} %broadcast_select_fusion.1), calls=%async_computation.1 | async-start | bytes 2097152 | tf_op jit(solution)/shard_map/all_to_all | solution.py:132
  218.3 664.6 %reduce-scatter.5.cloned.1.call-start = ((), (), s32[]{:S(2)}) async-start(), calls=%async_computation.5 | async-start | bytes 786432 | tf_op jit(solution)/shard_map/reduce_scatter | solution.py:203
  222.8 0.8 copy-start.4
  243.3 1.0 copy-start.5
  243.3 1.4 copy-start.6
  289.9 44.3 %copy-start.1 = (f32[16,128,128]{2,1,0:T(8,128)}, f32[16,128,128]{2,1,0:T(8,128)S(1)}, u32[]{:S(2)}) copy-start(f32[16,128,128]{2,1,0:T(8,128)S(1)} %get-tuple-element.903) | copy-start | bytes 3145732 | tf_op jit(solution)/shard_map/while
  334.2 1.2 copy-start.2
  593.1 44.3 %copy-start.1 = (f32[16,128,128]{2,1,0:T(8,128)}, f32[16,128,128]{2,1,0:T(8,128)S(1)}, u32[]{:S(2)}) copy-start(f32[16,128,128]{2,1,0:T(8,128)S(1)} %get-tuple-element.903) | copy-start | bytes 3145732 | tf_op jit(solution)/shard_map/while
  637.3 1.2 copy-start.2
  859.3 40.5 %reduce-scatter.3.cloned.1.call-start = ((), (), s32[]{:S(2)}) async-start(), calls=%async_computation.4 | async-start | bytes 786432 | tf_op jit(solution)/shard_map/reduce_scatter | solution.py:202
Sparse Core Ops, SparseCore 0:
  859.4 23.4 reduce-scatter.4
  885.2 14.5 reduce-scatter.2
where the time goes:
time: 917 us; the launch traced here: 909 us
  local copies, waits for them, and re-layouts  481 us (52%)
  loops' own time  245 us (27%)
  waiting for transfers between devices  58.2 us (6%)
  other arithmetic  44.6 us (5%)
  matrix products  31.1 us (3%)
  blocking collectives  21.1 us (2%)
  between operations  13.8 us (2%)
  starting transfers between devices  13.3 us (1%)
    gather x384, local copies, waits for them, and re-layouts  296 us
    another operation x4, loops' own time, accumulate(): return lax.fori_loop(0, contrib.shape[0], add_one, patch_grid)  243 us
    dynamic_update_slice x64, local copies, waits for them, and re-layouts, add_one(): lax.dynamic_update_slice(acc, current + contrib[item], (row_at, col_at))  114 us
    dynamic_slice x64, local copies, waits for them, and re-layouts, add_one(): col_at = offset_sel[1, item]  40.2 us
    add x64, other arithmetic, add_one(): current + contrib[item]  33.1 us
    reduce_scatter x1, waiting for transfers between devices, local(): lax.psum_scatter(slab_grads[1], 'cuts', scatter_dimension=0, tiled=True)  22.9 us
    dot_general x24, matrix products, right_product(): jnp.einsum('nab,bc->nac', field, matrix, preferred_element_type=jnp.float32)  19.9 us
  transfers between devices with their start and end apart: 4, of which 3 were waited for; matrix products, arithmetic and copies ran while one was open for 19% of the time, Pallas kernels for 0%

commit v1 on v0

v1 whole, which is shorter than its diff:
```python
import functools
import math

import jax
import jax.numpy as jnp
import ml_dtypes
import numpy as np
from jax import lax
from jax.experimental import pallas as pl
from jax.experimental.pallas import tpu as pltpu
from jax.sharding import PartitionSpec as P

fresnel_strength = 9.0
softening = 0.01
LANES = 128


def tables(extent):
    indices = np.arange(extent)
    angles = (indices[:, None] * indices[None, :] % extent) * (2.0 * math.pi / extent)
    wave = np.cos(angles) + 1j * np.sin(angles)
    frequency = np.where(indices < (extent + 1) // 2, indices, indices - extent) / extent
    kernel = np.exp(-1j * fresnel_strength * frequency * frequency)
    prop = (wave * kernel[None, :]) @ wave.conj() / extent
    four = wave.conj() / math.sqrt(extent)
    blocks = []
    for matrix in (prop, four):
        real, imag = matrix.real, matrix.imag
        blocks.append(np.block([[real, -imag], [imag, real]]))
        blocks.append(np.block([[real, imag], [-imag, real]]))
    return [b.astype(np.float32).astype(ml_dtypes.bfloat16) for b in blocks]


def apply_both(left, right, fields):
    extent = fields[0][0].shape[0]
    count = len(fields)
    cat = jnp.concatenate(
        [
            jnp.concatenate([f[0] for f in fields], axis=1),
            jnp.concatenate([f[1] for f in fields], axis=1),
        ],
        axis=0,
    )
    mid = jnp.dot(left, cat, preferred_element_type=jnp.float32).astype(jnp.bfloat16)
    rows = jnp.concatenate(
        [
            jnp.concatenate(
                [
                    mid[:extent, n * extent : (n + 1) * extent],
                    mid[extent:, n * extent : (n + 1) * extent],
                ],
                axis=1,
            )
            for n in range(count)
        ],
        axis=0,
    )
    end = jnp.dot(rows, right, preferred_element_type=jnp.float32)
    return [
        (
            end[n * extent : (n + 1) * extent, :extent],
            end[n * extent : (n + 1) * extent, extent:],
        )
        for n in range(count)
    ]


def kernel(
    tiles,
    slices,
    count,
    chunk,
    off_ref,
    own_ref,
    trr_ref,
    tri_ref,
    pr_ref,
    pi_ref,
    req_ref,
    meas_ref,
    lg_ref,
    rg_ref,
    lf_ref,
    rf_ref,
    out_ref,
    slab,
    tsend,
    trecv,
    rrecv,
    psend,
    pats,
    wins,
    psis,
    far,
    grads,
    pad,
    acc,
    gsend,
    grecv,
    ts_sem,
    tr_sem,
    rs_sem,
    rr_sem,
    ps_sem,
    pr_sem,
    gs_sem,
    gr_sem,
):
    extent = pr_ref.shape[0]
    height = trr_ref.shape[1]
    reach = height - extent
    halves = trr_ref.shape[2] // LANES
    cut = lax.axis_index("cuts")
    tile = lax.axis_index("tile")

    def tile_at(step):
        return {"tile": lax.rem(tile + step, tiles)}

    def cut_at(step):
        return {"cuts": lax.rem(cut + step, slices)}

    barrier = pltpu.get_barrier_semaphore()
    for step in range(1, tiles):
        pl.semaphore_signal(
            barrier, inc=1, device_id=tile_at(step), device_id_type=pl.DeviceIdType.MESH
        )
    for step in range(1, slices):
        pl.semaphore_signal(
            barrier, inc=1, device_id=cut_at(step), device_id_type=pl.DeviceIdType.MESH
        )

    def split_own(plane, ref):
        for half in range(halves):
            block = ref[0, :, half * LANES : (half + 1) * LANES]
            slab[cut, plane, half] = block
            tsend[plane, half] = block.astype(jnp.bfloat16)

    split_own(0, trr_ref)
    split_own(1, tri_ref)
    pl.semaphore_wait(barrier, tiles - 1 + slices - 1)

    def request_copy(step):
        return pltpu.make_async_remote_copy(
            src_ref=req_ref.at[lax.rem(tile + step, tiles)],
            dst_ref=rrecv.at[step],
            send_sem=rs_sem.at[step],
            recv_sem=rr_sem.at[step],
            device_id=tile_at(step),
            device_id_type=pl.DeviceIdType.MESH,
        )

    def slab_copy(step):
        return pltpu.make_async_remote_copy(
            src_ref=tsend,
            dst_ref=trecv.at[step - 1],
            send_sem=ts_sem.at[step - 1],
            recv_sem=tr_sem.at[step - 1],
            device_id=cut_at(step),
            device_id_type=pl.DeviceIdType.MESH,
        )

    def pattern_copy(step):
        return pltpu.make_async_remote_copy(
            src_ref=psend.at[step],
            dst_ref=pats.at[step],
            send_sem=ps_sem.at[step],
            recv_sem=pr_sem.at[step],
            device_id=tile_at(tiles - step),
            device_id_type=pl.DeviceIdType.MESH,
        )

    for step in range(1, tiles):
        request_copy(step).start()
    for step in range(1, slices):
        slab_copy(step).start()

    acc[...] = jnp.zeros_like(acc)
    pad[...] = jnp.zeros_like(pad)
    pats[0] = meas_ref[req_ref[tile][0, 0]]
    for step in range(1, tiles):
        request_copy(step).wait_recv()
        psend[step] = meas_ref[rrecv[step][0, 0]]
        pattern_copy(step).start()

    for step in range(1, slices):
        slab_copy(step).wait_recv()
        slab[lax.rem(cut + slices - step, slices)] = trecv[step - 1].astype(jnp.float32)

    lane = lax.broadcasted_iota(jnp.int32, (extent, LANES), 1)

    def window(layer, plane, row, col):
        low = slab[layer, plane, 0, pl.ds(row, extent), :]
        high = slab[layer, plane, 1, pl.ds(row, extent), :]
        return pltpu.roll(
            jnp.where(lane >= col, low, high), lax.rem(2 * LANES - col, LANES), axis=1
        )

    def descend(item, _):
        base = item * chunk
        probe = (pr_ref[...], pi_ref[...])
        waves = [probe] * chunk
        for layer in range(slices):
            fields = []
            for n in range(chunk):
                row, col = off_ref[0, base + n], off_ref[1, base + n]
                win_real = window(layer, 0, row, col)
                win_imag = window(layer, 1, row, col)
                if layer > 0:
                    wins[layer - 1, base + n, 0] = win_real
                    wins[layer - 1, base + n, 1] = win_imag
                    psis[layer - 1, base + n, 0] = waves[n][0]
                    psis[layer - 1, base + n, 1] = waves[n][1]
                wave_real = waves[n][0].astype(jnp.float32)
                wave_imag = waves[n][1].astype(jnp.float32)
                fields.append(
                    (
                        (win_real * wave_real - win_imag * wave_imag).astype(jnp.bfloat16),
                        (win_real * wave_imag + win_imag * wave_real).astype(jnp.bfloat16),
                    )
                )
            ends = apply_both(lg_ref[...], rg_ref[...], fields)
            waves = [(e[0].astype(jnp.bfloat16), e[1].astype(jnp.bfloat16)) for e in ends]
        ends = apply_both(lf_ref[...], rf_ref[...], waves)
        for n in range(chunk):
            far[base + n, 0] = ends[n][0]
            far[base + n, 1] = ends[n][1]
        return 0

    lax.fori_loop(0, count // chunk, descend, 0)

    for step in range(1, tiles):
        pattern_copy(step).wait_recv()

    def seeds(base):
        fields = []
        for n in range(chunk):
            owner = own_ref[0, base + n]
            amplitude = pats[lax.rem(owner - tile + tiles, tiles)].astype(jnp.float32)
            far_real = far[base + n, 0]
            far_imag = far[base + n, 1]
            inverse = lax.rsqrt(far_real * far_real + far_imag * far_imag + softening)
            ratio = 1.0 - amplitude * inverse
            fields.append(
                (
                    (ratio * far_real).astype(jnp.bfloat16),
                    (ratio * far_imag).astype(jnp.bfloat16),
                )
            )
        ends = apply_both(rf_ref[...], lf_ref[...], fields)
        return [(e[0].astype(jnp.bfloat16), e[1].astype(jnp.bfloat16)) for e in ends]

    def grad_copy(layer):
        step = lax.rem(layer - cut + slices, slices)
        return pltpu.make_async_remote_copy(
            src_ref=gsend.at[layer],
            dst_ref=grecv.at[step - 1],
            send_sem=gs_sem.at[layer],
            recv_sem=gr_sem.at[step - 1],
            device_id={"cuts": layer},
            device_id_type=pl.DeviceIdType.MESH,
        )

    for layer in reversed(range(slices)):

        def ascend(item, _):
            base = item * chunk
            if layer == slices - 1:
                fields = seeds(base)
            else:
                fields = [(grads[base + n, 0], grads[base + n, 1]) for n in range(chunk)]
            ends = apply_both(rg_ref[...], lg_ref[...], fields)
            for n in range(chunk):
                back_real, back_imag = ends[n]
                col = off_ref[1, base + n]
                if layer > 0:
                    psi_real = psis[layer - 1, base + n, 0].astype(jnp.float32)
                    psi_imag = psis[layer - 1, base + n, 1].astype(jnp.float32)
                    win_real = wins[layer - 1, base + n, 0]
                    win_imag = wins[layer - 1, base + n, 1]
                    grads[base + n, 0] = (back_real * win_real + back_imag * win_imag).astype(
                        jnp.bfloat16
                    )
                    grads[base + n, 1] = (back_imag * win_real - back_real * win_imag).astype(
                        jnp.bfloat16
                    )
                else:
                    psi_real = pr_ref[...].astype(jnp.float32)
                    psi_imag = pi_ref[...].astype(jnp.float32)
                terms = (
                    back_real * psi_real + back_imag * psi_imag,
                    back_imag * psi_real - back_real * psi_imag,
                )
                for plane in range(2):
                    rolled = pltpu.roll(terms[plane], lax.rem(col, LANES), axis=1)
                    pad[n, plane, 0, reach : reach + extent] = jnp.where(lane >= col, rolled, 0.0)
                    pad[n, plane, 1, reach : reach + extent] = jnp.where(lane < col, rolled, 0.0)
            for plane in range(2):
                for half in range(2):
                    total = acc[layer, plane, half]
                    for n in range(chunk):
                        start = reach - off_ref[0, base + n]
                        total = total + pad[n, plane, half, pl.ds(start, height), :]
                    acc[layer, plane, half] = total
            return 0

        lax.fori_loop(0, count // chunk, ascend, 0)

        @pl.when(cut != layer)
        def _():
            gsend[layer] = acc[layer].astype(jnp.bfloat16)
            grad_copy(layer).start()

    for step in range(1, slices):
        pltpu.make_async_remote_copy(
            src_ref=gsend.at[0],
            dst_ref=grecv.at[step - 1],
            send_sem=gs_sem.at[0],
            recv_sem=gr_sem.at[step - 1],
            device_id=cut_at(step),
            device_id_type=pl.DeviceIdType.MESH,
        ).wait_recv()
    for plane in range(2):
        for half in range(2):
            total = acc[cut, plane, half]
            for step in range(1, slices):
                total = total + grecv[step - 1, plane, half].astype(jnp.float32)
            out_ref[plane, 0, :, half * LANES : (half + 1) * LANES] = total

    for step in range(1, tiles):
        request_copy(step).wait_send()
        pattern_copy(step).wait_send()
    for step in range(1, slices):
        slab_copy(step).wait_send()
    for layer in range(slices):

        @pl.when(cut != layer)
        def _():
            grad_copy(layer).wait_send()


def local(trans_real, trans_imag, probe_real, probe_imag, offsets, pattern_index, measured):
    extent = probe_real.shape[-1]
    positions = pattern_index.shape[0]
    tiles = lax.axis_size("tile")
    slices = lax.axis_size("cuts")
    cut = lax.axis_index("cuts")
    height, width = trans_real.shape[1:]
    assert extent == LANES and width == 2 * LANES and trans_real.shape[0] == 1
    assert positions % slices == 0
    assert (positions + tiles - 1) // tiles <= slices
    count = positions // slices
    chunk = math.gcd(count, 4)

    owners = pattern_index // positions
    slots = pattern_index % positions
    order_key = owners * positions + jnp.arange(positions, dtype=jnp.int32)
    ordinal = jnp.sum((order_key[None, :] < order_key[:, None]).astype(jnp.int32), axis=1)
    places = jnp.arange(count, dtype=jnp.int32) * slices + cut
    hit = (places[:, None] == ordinal[None, :]).astype(jnp.int32)
    off_mine = jnp.sum(hit[None] * offsets[:, None, :], axis=2)
    own_mine = jnp.sum(hit * owners[None, :], axis=1)[None]
    wanted = (owners[None, :] == jnp.arange(tiles, dtype=jnp.int32)[:, None]) & (
        lax.rem(ordinal, slices) == cut
    )[None, :]
    request = jnp.sum(jnp.where(wanted, slots[None, :], 0), axis=1)
    request = jnp.broadcast_to(request[:, None, None], (tiles, 1, LANES))

    blocks = [jnp.asarray(b) for b in tables(extent)]
    others = max(slices - 1, 1)
    bf16, f32 = jnp.bfloat16, jnp.float32
    vmem = pl.BlockSpec(memory_space=pltpu.VMEM)
    smem = pl.BlockSpec(memory_space=pltpu.SMEM)
    dma = pltpu.SemaphoreType.DMA
    return pl.pallas_call(
        functools.partial(kernel, tiles, slices, count, chunk),
        out_shape=jax.ShapeDtypeStruct((2, 1, height, width), f32),
        in_specs=[smem, smem] + [vmem] * 10,
        out_specs=vmem,
        scratch_shapes=[
            pltpu.VMEM((slices, 2, 2, height, LANES), f32),
            pltpu.VMEM((2, 2, height, LANES), bf16),
            pltpu.VMEM((others, 2, 2, height, LANES), bf16),
            pltpu.VMEM((tiles, 1, LANES), jnp.int32),
            pltpu.VMEM((tiles, extent, extent), bf16),
            pltpu.VMEM((tiles, extent, extent), bf16),
            pltpu.VMEM((others, count, 2, extent, extent), f32),
            pltpu.VMEM((others, count, 2, extent, extent), bf16),
            pltpu.VMEM((count, 2, extent, extent), f32),
            pltpu.VMEM((count, 2, extent, extent), bf16),
            pltpu.VMEM((chunk, 2, 2, 2 * height - extent, LANES), f32),
            pltpu.VMEM((slices, 2, 2, height, LANES), f32),
            pltpu.VMEM((slices, 2, 2, height, LANES), bf16),
            pltpu.VMEM((others, 2, 2, height, LANES), bf16),
            dma((others,)),
            dma((others,)),
            dma((tiles,)),
            dma((tiles,)),
            dma((tiles,)),
            dma((tiles,)),
            dma((slices,)),
            dma((others,)),
        ],
        compiler_params=pltpu.CompilerParams(
            collective_id=0, has_side_effects=True, vmem_limit_bytes=56 * 1024 * 1024
        ),
    )(off_mine, own_mine, trans_real, trans_imag, probe_real, probe_imag, request, measured, *blocks)


def solution(mesh):
    return jax.shard_map(
        local,
        mesh=mesh,
        in_specs=(
            P("cuts", "tile", None),
            P("cuts", "tile", None),
            P(),
            P(),
            P(None, "tile"),
            P("tile"),
            P("tile", None, None),
        ),
        out_specs=P(None, "cuts", "tile", None),
        check_vma=False,
    )
```

time: 917 us -> 45.2 us (0.05)
  local copies, waits for them, and re-layouts: 481 us -> 3.81 us
  loops' own time: 245 us -> 0 us
  waiting for transfers between devices: 58.2 us -> 0 us
  other arithmetic: 44.6 us -> 1.68 us
  Pallas kernels: 0 us -> 39.4 us
  matrix products: 31.1 us -> 0 us
  blocking collectives: 21.1 us -> 0 us
  between operations: 13.8 us -> 0.02 us
  starting transfers between devices: 13.3 us -> 0 us
    gather x386 -> x0, local copies, waits for them, and re-layouts: 299 us -> none
    another operation x14 -> x0, loops' own time: 245 us -> none  [the longest x4 243 us: accumulate(): return lax.fori_loop(0, contrib.shape[0], add_one, patch_grid)]
    dynamic_update_slice x68 -> x0, local copies, waits for them, and re-layouts: 118 us -> none  [the longest x64 114 us: add_one(): lax.dynamic_update_slice(acc, current + contrib[item], (row_at, col_at))]
    dynamic_slice x66 -> x0, local copies, waits for them, and re-layouts: 40.2 us -> none  [the longest x64 40.2 us: add_one(): col_at = offset_sel[1, item]]
    reduce_scatter x2 -> x0, waiting for transfers between devices: 39.8 us -> none  [the longest x1 22.9 us: local(): lax.psum_scatter(slab_grads[1], 'cuts', scatter_dimension=0, tiled=True)]
    pallas_call x0 -> x1, Pallas kernels: none -> 39.4 us  [local(): pl.pallas_call(functools.partial(kernel, tiles, slices, count, chunk), ou...]
    add x64 -> x2, other arithmetic: 33.1 us -> 0.02 us  [the longest x1 0.01 us: local(): order_key = owners * positions + jnp.arange(positions, dtype=jnp.int32)]
    dot_general x52 -> x0, matrix products: 31.1 us -> none  [the longest x24 19.9 us: right_product(): jnp.einsum('nab,bc->nac', field, matrix, preferred_element_type=jnp.float32)]
  transfers between devices with their start and end apart: 4 -> 0, of which waited for: 3 -> 0; matrix products, arithmetic and copies ran while one was open for 19% -> 0% of each run, Pallas kernels for 0% -> 0%
where the time goes in v1:
time: 45.2 us; the launch traced here: 44.9 us
  Pallas kernels  39.4 us (87%)
  local copies, waits for them, and re-layouts  3.81 us (8%)
  other arithmetic  1.68 us (4%)
    pallas_call x1, Pallas kernels, local(): pl.pallas_call(functools.partial(kernel, tiles, slices, count, chunk), ou...  39.4 us
    unnamed x5, local copies, waits for them, and re-layouts  3.13 us

profile of v1, /device:TPU:0, one launch (start us, length us, event | category | flops | bytes accessed | tf_op | source)
XLA Modules:
  0.0 44.9 jit_solution(12216769284919287864)
XLA Ops:
  0.0 0.0 copy-start.1
  0.0 0.6 %copy-done.1 = s32[32]{0:T(128)S(1)} copy-done((s32[32]{0:T(128)S(1)}, s32[32]{0:T(128)}, u32[]{:S(2)}) %copy-start.1) | copy-done | bytes 152
  0.7 0.2 convert_reduce_fusion
  0.9 0.7 %select_reduce_fusion = (s32[16]{0:T(128)S(1)}, s32[16]{0:T(128)}) fusion(s32[32]{0:T(128)S(1)} %get-tuple-element.9, s32[32]{0:T(128)S(1)} %get-tuple-element.8, pred[32]{0:T(512)(128)(4,1)S(1)} %fusion.3, s32[32]{0:T(128)S(1)} %convert_reduce_fusion, s32[16]{0:T(128)S(1)} %multiply_add_fusion), kind=kLoop, calls=%fused_computation.5 | loop fusion | flops 3552 | bytes 608 | tf_op jit(solution)/shard_map/reduce_sum | solution.py:365
  1.6 0.0 copy-start
  1.6 0.1 compare_convert_fusion
  1.6 0.6 %copy-done = s32[2,32]{1,0:T(2,128)S(1)} copy-done((s32[2,32]{1,0:T(2,128)S(1)}, s32[2,32]{1,0:T(2,128)}, u32[]{:S(2)}) %copy-start) | copy-done | bytes 280
  2.2 0.7 %multiply_reduce_fusion.off_ref = s32[2,16]{1,0:T(2,128)} fusion(s32[2,32]{1,0:T(2,128)S(1)} %copy-done, s32[16,32]{1,0:T(8,128)S(1)} %compare_convert_fusion), kind=kLoop, calls=%fused_computation | loop fusion | flops 2016 | bytes 2432 | tf_op jit(solution)/shard_map/reduce_sum | solution.py:360
  2.9 0.7 %broadcast_in_dim.12.req_ref = s32[16,1,128]{2,1,0:T(1,128)} broadcast(s32[16]{0:T(128)S(1)} %get-tuple-element.5), dimensions={0} | broadcast | bytes 8256 | tf_op jit(solution)/shard_map/broadcast_in_dim | solution.py:366
  3.6 39.4 %shard_map.109 = f32[2,1,256,256]{3,2,1,0:T(8,128)} custom-call(s32[2,16]{1,0:T(2,128)} %multiply_reduce_fusion.off_ref, s32[1,16]{1,0:T(1,128)} %bitcast.1, f32[1,256,256]{2,1,0:T(8,128)} %trr_ref.1, f32[1,256,256]{2,1,0:T(8,128)} %tri_ref.1, bf16[128,128]{1,0:T(8,128)(2,1)} %pr_ref.1, bf16[128,128]{1,0:T(8,128)(2,1)} %pi_ref.1, ...), custom_call_target="tpu_custom_call" | custom-call | tf_op jit(solution)/shard_map/pallas_call | solution.py:374
  43.1 1.9 %copy.13 = f32[2,1,256,256]{3,2,1,0:T(8,128)} copy(f32[2,1,256,256]{3,2,1,0:T(8,128)} %shard_map.109) | data formatting | bytes 1048576
  (3 shorter events, 0.0 us)
Async XLA Ops:
  0.0 0.7 %copy-start.1 = (s32[32]{0:T(128)S(1)}, s32[32]{0:T(128)}, u32[]{:S(2)}) copy-start(s32[32]{0:T(128)} %param.16) | copy-start | bytes 388
  1.6 0.7 %copy-start = (s32[2,32]{1,0:T(2,128)S(1)}, s32[2,32]{1,0:T(2,128)}, u32[]{:S(2)}) copy-start(s32[2,32]{1,0:T(2,128)} %param.15) | copy-start | bytes 772

commit v2 on v1

v2 whole, which is shorter than its diff:
```python
import functools
import math

import jax
import jax.numpy as jnp
import ml_dtypes
import numpy as np
from jax import lax
from jax.experimental import pallas as pl
from jax.experimental.pallas import tpu as pltpu
from jax.sharding import PartitionSpec as P

fresnel_strength = 9.0
softening = 0.01
LANES = 128


def tables(extent):
    indices = np.arange(extent)
    angles = (indices[:, None] * indices[None, :] % extent) * (2.0 * math.pi / extent)
    wave = np.cos(angles) + 1j * np.sin(angles)
    frequency = np.where(indices < (extent + 1) // 2, indices, indices - extent) / extent
    kernel = np.exp(-1j * fresnel_strength * frequency * frequency)
    prop = (wave * kernel[None, :]) @ wave.conj() / extent
    four = wave.conj() / math.sqrt(extent)
    blocks = []
    for matrix in (prop, four):
        real, imag = matrix.real, matrix.imag
        blocks.append(np.block([[real, -imag], [imag, real]]))
        blocks.append(np.block([[real, imag], [-imag, real]]))
    return [b.astype(np.float32).astype(ml_dtypes.bfloat16) for b in blocks]


def apply_both(left, right, fields):
    extent = fields[0][0].shape[0]
    count = len(fields)
    cat = jnp.concatenate(
        [
            jnp.concatenate([f[0] for f in fields], axis=1),
            jnp.concatenate([f[1] for f in fields], axis=1),
        ],
        axis=0,
    )
    mid = jnp.dot(left, cat, preferred_element_type=jnp.float32).astype(jnp.bfloat16)
    rows = jnp.concatenate(
        [
            jnp.concatenate(
                [
                    mid[:extent, n * extent : (n + 1) * extent],
                    mid[extent:, n * extent : (n + 1) * extent],
                ],
                axis=1,
            )
            for n in range(count)
        ],
        axis=0,
    )
    end = jnp.dot(rows, right, preferred_element_type=jnp.float32)
    return [
        (
            end[n * extent : (n + 1) * extent, :extent],
            end[n * extent : (n + 1) * extent, extent:],
        )
        for n in range(count)
    ]


def exclusive_or(first, second, size):
    result, unit = 0, 1
    while unit < size:
        one, two = first // unit % 2, second // unit % 2
        result = result + (one + two - 2 * one * two) * unit
        unit *= 2
    return result


def kernel(
    tiles,
    slices,
    count,
    chunk,
    exact,
    off_ref,
    index_ref,
    pr_ref,
    pi_ref,
    trr_ref,
    tri_ref,
    meas_hbm,
    table_hbm,
    own_out,
    recv_out,
    meas,
    table,
    place,
    source,
    qsend,
    slab,
    tsend,
    trecv,
    rrecv,
    psend,
    pats,
    wins,
    psis,
    far,
    pad,
    acc,
    gsend,
    in_sem,
    ts_sem,
    tr_sem,
    rs_sem,
    rr_sem,
    ps_sem,
    pr_sem,
    gs_sem,
    gr_sem,
    own_sem,
):
    extent = pr_ref.shape[0]
    height = trr_ref.shape[1]
    positions = index_ref.shape[1]
    reach = height - extent
    cut = lax.axis_index("cuts")
    tile = lax.axis_index("tile")
    mesh_ids = pl.DeviceIdType.MESH

    def peer(step):
        return exclusive_or(tile, step, tiles)

    def cut_at(step):
        return {"cuts": lax.rem(cut + step, slices)}

    barrier = pltpu.get_barrier_semaphore()
    near = list(range(1, tiles // 2))
    order = []
    for step in range(tiles // 2, tiles):
        order.append(step)
        if near:
            order.append(near.pop(0))
    for step in order:
        pl.semaphore_signal(
            barrier, inc=1, device_id={"tile": peer(step)}, device_id_type=mesh_ids
        )
    for step in range(1, slices):
        pl.semaphore_signal(barrier, inc=1, device_id=cut_at(step), device_id_type=mesh_ids)

    slab_in = [
        pltpu.make_async_copy(
            ref.at[0, :, pl.ds(half * LANES, LANES)],
            slab.at[cut, plane, half],
            in_sem.at[2 + 2 * plane + half],
        )
        for plane, ref in enumerate((trr_ref, tri_ref))
        for half in range(2)
    ]
    meas_in = pltpu.make_async_copy(meas_hbm, meas, in_sem.at[0])
    table_in = pltpu.make_async_copy(table_hbm, table, in_sem.at[1])
    for copy in slab_in:
        copy.start()
    meas_in.start()
    table_in.start()

    wanted = index_ref[...]
    lanes = lax.broadcasted_iota(jnp.int32, (1, positions), 1)
    key_row = jnp.broadcast_to(wanted // positions * positions + lanes, (positions, positions))
    diagonal = lax.broadcasted_iota(jnp.int32, (positions, positions), 0) == (
        lax.broadcasted_iota(jnp.int32, (positions, positions), 1)
    )
    key_col = jnp.sum(jnp.where(diagonal, key_row, 0), axis=1, keepdims=True)
    ordinal = jnp.sum(jnp.where(key_col < key_row, 1, 0), axis=0, keepdims=True)
    asked = jnp.where(lax.rem(ordinal, slices) == cut, wanted, -1)
    qsend[...] = jnp.full_like(qsend, -1)
    qsend[:, :positions] = asked

    for copy in slab_in:
        copy.wait()
    for plane in range(2):
        for half in range(2):
            tsend[plane, half] = slab[cut, plane, half].astype(jnp.bfloat16)
    pl.semaphore_wait(barrier, tiles - 1 + slices - 1)

    def request_copy(step):
        return pltpu.make_async_remote_copy(
            src_ref=qsend,
            dst_ref=rrecv.at[step],
            send_sem=rs_sem.at[step],
            recv_sem=rr_sem.at[step],
            device_id={"tile": peer(step)},
            device_id_type=mesh_ids,
        )

    def slab_copy(step):
        return pltpu.make_async_remote_copy(
            src_ref=tsend,
            dst_ref=trecv.at[step - 1],
            send_sem=ts_sem.at[step - 1],
            recv_sem=tr_sem.at[step - 1],
            device_id=cut_at(step),
            device_id_type=mesh_ids,
        )

    def pattern_copy(step):
        return pltpu.make_async_remote_copy(
            src_ref=psend.at[step],
            dst_ref=pats.at[step],
            send_sem=ps_sem.at[step],
            recv_sem=pr_sem.at[step],
            device_id={"tile": peer(step)},
            device_id_type=mesh_ids,
        )

    def pattern_for(row):
        slot = row - tile * positions
        slot = jnp.max(jnp.where((slot >= 0) & (slot < positions), slot, 0))
        return meas[slot]

    for step in order:
        request_copy(step).start()
    for step in range(1, slices):
        slab_copy(step).start()
    for item in range(count):
        owner = peer(item) if exact else item
        match = ordinal == owner * slices + cut
        place[item] = jnp.max(jnp.where(match, lanes, 0))
        if not exact:
            owner = jnp.max(jnp.where(match, wanted, 0)) // positions
            source[item] = exclusive_or(tile, owner, tiles)
    meas_in.wait()
    for step in order:
        request_copy(step).wait_recv()
        psend[step] = pattern_for(rrecv[step])
        pattern_copy(step).start()
    pats[0] = pattern_for(qsend[...])
    acc[...] = jnp.zeros_like(acc)
    pad[...] = jnp.zeros_like(pad)
    table_in.wait()

    for step in range(1, slices):
        slab_copy(step).wait_recv()
        slab[lax.rem(cut + slices - step, slices)] = trecv[step - 1].astype(jnp.float32)

    lane = lax.broadcasted_iota(jnp.int32, (extent, LANES), 1)

    def window(layer, plane, row, col):
        low = slab[layer, plane, 0, pl.ds(row, extent), :]
        high = slab[layer, plane, 1, pl.ds(row, extent), :]
        return pltpu.roll(
            jnp.where(lane >= col, low, high), lax.rem(2 * LANES - col, LANES), axis=1
        )

    def descend(item, _):
        base = item * chunk
        waves = [(pr_ref[...], pi_ref[...])] * chunk
        for layer in range(slices):
            fields = []
            for n in range(chunk):
                at = place[base + n]
                row, col = off_ref[0, at], off_ref[1, at]
                win_real = window(layer, 0, row, col)
                win_imag = window(layer, 1, row, col)
                if layer > 0:
                    wins[layer - 1, base + n, 0] = win_real
                    wins[layer - 1, base + n, 1] = win_imag
                    psis[layer - 1, base + n, 0] = waves[n][0]
                    psis[layer - 1, base + n, 1] = waves[n][1]
                wave_real = waves[n][0].astype(jnp.float32)
                wave_imag = waves[n][1].astype(jnp.float32)
                fields.append(
                    (
                        (win_real * wave_real - win_imag * wave_imag).astype(jnp.bfloat16),
                        (win_real * wave_imag + win_imag * wave_real).astype(jnp.bfloat16),
                    )
                )
            ends = apply_both(table[0], table[1], fields)
            waves = [(e[0].astype(jnp.bfloat16), e[1].astype(jnp.bfloat16)) for e in ends]
        ends = apply_both(table[2], table[3], waves)
        for n in range(chunk):
            far[base + n, 0] = ends[n][0]
            far[base + n, 1] = ends[n][1]
        return 0

    lax.fori_loop(0, count // chunk, descend, 0)

    if not exact:
        for step in order:
            pattern_copy(step).wait_recv()

    def seeds(base):
        fields = []
        for n in range(chunk):
            at = base + n if exact else source[base + n]
            amplitude = pats[at].astype(jnp.float32)
            far_real = far[base + n, 0]
            far_imag = far[base + n, 1]
            inverse = lax.rsqrt(far_real * far_real + far_imag * far_imag + softening)
            ratio = 1.0 - amplitude * inverse
            fields.append(
                (
                    (ratio * far_real).astype(jnp.bfloat16),
                    (ratio * far_imag).astype(jnp.bfloat16),
                )
            )
        ends = apply_both(table[3], table[2], fields)
        return [(e[0].astype(jnp.bfloat16), e[1].astype(jnp.bfloat16)) for e in ends]

    def grad_copy(layer, step, plane, half, target):
        return pltpu.make_async_remote_copy(
            src_ref=gsend.at[layer, plane, half],
            dst_ref=recv_out.at[step - 1, plane, :, pl.ds(half * LANES, LANES)],
            send_sem=gs_sem.at[layer, plane, half],
            recv_sem=gr_sem.at[step - 1, plane, half],
            device_id={"cuts": target},
            device_id_type=mesh_ids,
        )

    def grad_to(layer, plane, half):
        return grad_copy(layer, lax.rem(layer - cut + slices, slices), plane, half, layer)

    def own_copy(layer, plane, half):
        return pltpu.make_async_copy(
            acc.at[layer, plane, half],
            own_out.at[plane, 0, :, pl.ds(half * LANES, LANES)],
            own_sem.at[plane, half],
        )

    chunks = count // chunk

    def ascend(item, _):
        base = item * chunk
        if exact:
            for n in range(chunk):

                @pl.when(base + n > 0)
                def _():
                    pattern_copy(base + n).wait_recv()

        fields = seeds(base)
        for layer in reversed(range(slices)):
            ends = apply_both(table[1], table[0], fields)
            fields = []
            for n in range(chunk):
                back_real, back_imag = ends[n]
                col = off_ref[1, place[base + n]]
                if layer > 0:
                    psi_real = psis[layer - 1, base + n, 0].astype(jnp.float32)
                    psi_imag = psis[layer - 1, base + n, 1].astype(jnp.float32)
                    win_real = wins[layer - 1, base + n, 0]
                    win_imag = wins[layer - 1, base + n, 1]
                    fields.append(
                        (
                            (back_real * win_real + back_imag * win_imag).astype(jnp.bfloat16),
                            (back_imag * win_real - back_real * win_imag).astype(jnp.bfloat16),
                        )
                    )
                else:
                    psi_real = pr_ref[...].astype(jnp.float32)
                    psi_imag = pi_ref[...].astype(jnp.float32)
                terms = (
                    back_real * psi_real + back_imag * psi_imag,
                    back_imag * psi_real - back_real * psi_imag,
                )
                for plane in range(2):
                    rolled = pltpu.roll(terms[plane], lax.rem(col, LANES), axis=1)
                    pad[n, plane, 0, reach : reach + extent] = jnp.where(lane >= col, rolled, 0.0)
                    pad[n, plane, 1, reach : reach + extent] = jnp.where(lane < col, rolled, 0.0)
            for plane in range(2):
                for half in range(2):
                    total = acc[layer, plane, half]
                    for n in range(chunk):
                        start = reach - off_ref[0, place[base + n]]
                        total = total + pad[n, plane, half, pl.ds(start, height), :]
                    acc[layer, plane, half] = total

                    @pl.when((item == chunks - 1) & (cut != layer))
                    def _():
                        gsend[layer, plane, half] = acc[layer, plane, half].astype(jnp.bfloat16)
                        grad_to(layer, plane, half).start()

                    @pl.when((item == chunks - 1) & (cut == layer))
                    def _():
                        own_copy(layer, plane, half).start()

        return 0

    lax.fori_loop(0, chunks, ascend, 0)

    for step in order:
        request_copy(step).wait_send()
        pattern_copy(step).wait_send()
    for step in range(1, slices):
        slab_copy(step).wait_send()
    for plane in range(2):
        for half in range(2):
            own_copy(cut, plane, half).wait()
            for layer in range(slices):

                @pl.when(cut != layer)
                def _():
                    grad_to(layer, plane, half).wait_send()

            for step in range(1, slices):
                grad_copy(0, step, plane, half, lax.rem(cut + step, slices)).wait_recv()


def local(trans_real, trans_imag, probe_real, probe_imag, offsets, pattern_index, measured):
    extent = probe_real.shape[-1]
    positions = pattern_index.shape[0]
    tiles = lax.axis_size("tile")
    slices = lax.axis_size("cuts")
    height, width = trans_real.shape[1:]
    assert extent == LANES and width == 2 * LANES and trans_real.shape[0] == 1
    assert positions % slices == 0 and positions <= LANES
    assert tiles & (tiles - 1) == 0
    assert (positions + tiles - 1) // tiles <= slices
    count = positions // slices
    chunk = math.gcd(count, 4)
    exact = count == tiles

    others = slices - 1
    bf16, f32 = jnp.bfloat16, jnp.float32
    vmem = pl.BlockSpec(memory_space=pltpu.VMEM)
    smem = pl.BlockSpec(memory_space=pltpu.SMEM)
    hbm = pl.BlockSpec(memory_space=pl.ANY)
    dma = pltpu.SemaphoreType.DMA
    own, received = pl.pallas_call(
        functools.partial(kernel, tiles, slices, count, chunk, exact),
        out_shape=(
            jax.ShapeDtypeStruct((2, 1, height, width), f32),
            jax.ShapeDtypeStruct((others, 2, height, width), bf16),
        ),
        in_specs=[smem, vmem, vmem, vmem, hbm, hbm, hbm, hbm],
        out_specs=(hbm, hbm),
        scratch_shapes=[
            pltpu.VMEM(measured.shape, bf16),
            pltpu.VMEM((4, 2 * extent, 2 * extent), bf16),
            pltpu.SMEM((count,), jnp.int32),
            pltpu.SMEM((count,), jnp.int32),
            pltpu.VMEM((1, LANES), jnp.int32),
            pltpu.VMEM((slices, 2, 2, height, LANES), f32),
            pltpu.VMEM((2, 2, height, LANES), bf16),
            pltpu.VMEM((others, 2, 2, height, LANES), bf16),
            pltpu.VMEM((tiles, 1, LANES), jnp.int32),
            pltpu.VMEM((tiles, extent, extent), bf16),
            pltpu.VMEM((tiles, extent, extent), bf16),
            pltpu.VMEM((others, count, 2, extent, extent), f32),
            pltpu.VMEM((others, count, 2, extent, extent), bf16),
            pltpu.VMEM((count, 2, extent, extent), f32),
            pltpu.VMEM((chunk, 2, 2, 2 * height - extent, LANES), f32),
            pltpu.VMEM((slices, 2, 2, height, LANES), f32),
            pltpu.VMEM((slices, 2, 2, height, LANES), bf16),
            dma((6,)),
            dma((others,)),
            dma((others,)),
            dma((tiles,)),
            dma((tiles,)),
            dma((tiles,)),
            dma((tiles,)),
            dma((slices, 2, 2)),
            dma((others, 2, 2)),
            dma((2, 2)),
        ],
        compiler_params=pltpu.CompilerParams(
            collective_id=0, has_side_effects=True, vmem_limit_bytes=56 * 1024 * 1024
        ),
    )(
        offsets,
        pattern_index[None],
        probe_real,
        probe_imag,
        trans_real,
        trans_imag,
        measured,
        jnp.asarray(np.stack(tables(extent))),
    )
    return own + jnp.sum(received.astype(f32), axis=0)[:, None]


def solution(mesh):
    return jax.shard_map(
        local,
        mesh=mesh,
        in_specs=(
            P("cuts", "tile", None),
            P("cuts", "tile", None),
            P(),
            P(),
            P(None, "tile"),
            P("tile"),
            P("tile", None, None),
        ),
        out_specs=P(None, "cuts", "tile", None),
        check_vma=False,
    )
```

time: 45.2 us -> 37.2 us (0.82)
  Pallas kernels: 39.4 us -> 35.1 us
  local copies, waits for them, and re-layouts: 3.81 us -> 0 us
    pallas_call x1, Pallas kernels: 39.4 us -> 35.1 us  [local(): pl.pallas_call(functools.partial(kernel, tiles, slices, count, chunk, exa...]
    unnamed x5 -> x0, local copies, waits for them, and re-layouts: 3.13 us -> none
    add x2 -> x1, other arithmetic: 0.02 us -> 1.96 us  [local(): return own + jnp.sum(received.astype(f32), axis=0)[:, None]]
    reduce_sum x3 -> x0, other arithmetic: 1.58 us -> none  [the longest x1 0.71 us: local(): off_mine = jnp.sum(hit[None] * offsets[:, None, :], axis=2)]
    broadcast_in_dim x1 -> x0, local copies, waits for them, and re-layouts: 0.68 us -> none  [local(): request = jnp.broadcast_to(request[:, None, None], (tiles, 1, LANES))]
where the time goes in v2:
time: 37.2 us; the launch traced here: 37 us
  Pallas kernels  35.1 us (94%)
  other arithmetic  1.96 us (5%)
    pallas_call x1, Pallas kernels, local(): pl.pallas_call(functools.partial(kernel, tiles, slices, count, chunk, exa...  35.1 us
    add x1, other arithmetic, local(): return own + jnp.sum(received.astype(f32), axis=0)[:, None]  1.96 us

profile of v2, /device:TPU:0, one launch (start us, length us, event | category | flops | bytes accessed | tf_op | source)
XLA Modules:
  0.0 37.0 jit_solution(14931485785504225760)
XLA Ops:
  0.0 35.1 %shard_map.82 = (f32[2,1,256,256]{3,2,1,0:T(8,128)}, bf16[1,2,256,256]{3,2,1,0:T(8,128)(2,1)}) custom-call(s32[2,32]{1,0:T(2,128)} %off_ref.1, s32[1,32]{1,0:T(1,128)} %bitcast.8, bf16[128,128]{1,0:T(8,128)(2,1)} %pr_ref.1, bf16[128,128]{1,0:T(8,128)(2,1)} %pi_ref.1, f32[1,256,256]{2,1,0:T(8,128)} %trr_ref.1, f32[1,256,256]{2,1,0:T(8,128)} %tri_ref.1, ...), custom_call_target="tpu_custom_call" | custom-call | tf_op jit(solution)/shard_map/pallas_call | solution.py:427
  35.1 2.0 %fusion = f32[2,1,256,256]{3,2,1,0:T(8,128)} fusion(f32[2,1,256,256]{3,2,1,0:T(8,128)} %get-tuple-element.7, bf16[1,2,256,256]{3,2,1,0:T(8,128)(2,1)} %get-tuple-element.8), kind=kLoop, calls=%fused_computation.1 | loop fusion | flops 262144 | bytes 1310720 | tf_op jit(solution)/shard_map/add | solution.py:477

commit v3 on v2

--- a/solution.py
+++ b/solution.py
@@ -250,12 +250,14 @@
             jnp.where(lane >= col, low, high), lax.rem(2 * LANES - col, LANES), axis=1
         )
 
+    wide = math.gcd(count, 8)
+
     def descend(item, _):
-        base = item * chunk
-        waves = [(pr_ref[...], pi_ref[...])] * chunk
+        base = item * wide
+        waves = [(pr_ref[...], pi_ref[...])] * wide
         for layer in range(slices):
             fields = []
-            for n in range(chunk):
+            for n in range(wide):
                 at = place[base + n]
                 row, col = off_ref[0, at], off_ref[1, at]
                 win_real = window(layer, 0, row, col)
@@ -276,12 +278,12 @@
             ends = apply_both(table[0], table[1], fields)
             waves = [(e[0].astype(jnp.bfloat16), e[1].astype(jnp.bfloat16)) for e in ends]
         ends = apply_both(table[2], table[3], waves)
-        for n in range(chunk):
+        for n in range(wide):
             far[base + n, 0] = ends[n][0]
             far[base + n, 1] = ends[n][1]
         return 0
 
-    lax.fori_loop(0, count // chunk, descend, 0)
+    lax.fori_loop(0, count // wide, descend, 0)
 
     if not exact:
         for step in order:

time: 37.2 us -> 36.2 us (0.973)
  Pallas kernels: 35.1 us -> 34.1 us
    pallas_call x1, Pallas kernels: 35.1 us -> 34.1 us  [local(): pl.pallas_call(functools.partial(kernel, tiles, slices, count, chunk, exa...]
where the time goes in v3:
time: 36.2 us; the launch traced here: 36 us
  Pallas kernels  34.1 us (94%)
  other arithmetic  1.96 us (5%)
    pallas_call x1, Pallas kernels, local(): pl.pallas_call(functools.partial(kernel, tiles, slices, count, chunk, exa...  34.1 us
    add x1, other arithmetic, local(): return own + jnp.sum(received.astype(f32), axis=0)[:, None]  1.96 us

profile of v3, /device:TPU:0, one launch (start us, length us, event | category | flops | bytes accessed | tf_op | source)
XLA Modules:
  0.0 36.0 jit_solution(16347346621369735467)
XLA Ops:
  0.0 34.1 %shard_map.82 = (f32[2,1,256,256]{3,2,1,0:T(8,128)}, bf16[1,2,256,256]{3,2,1,0:T(8,128)(2,1)}) custom-call(s32[2,32]{1,0:T(2,128)} %off_ref.1, s32[1,32]{1,0:T(1,128)} %bitcast.8, bf16[128,128]{1,0:T(8,128)(2,1)} %pr_ref.1, bf16[128,128]{1,0:T(8,128)(2,1)} %pi_ref.1, f32[1,256,256]{2,1,0:T(8,128)} %trr_ref.1, f32[1,256,256]{2,1,0:T(8,128)} %tri_ref.1, ...), custom_call_target="tpu_custom_call" | custom-call | tf_op jit(solution)/shard_map/pallas_call | solution.py:429
  34.1 2.0 %fusion = f32[2,1,256,256]{3,2,1,0:T(8,128)} fusion(f32[2,1,256,256]{3,2,1,0:T(8,128)} %get-tuple-element.7, bf16[1,2,256,256]{3,2,1,0:T(8,128)(2,1)} %get-tuple-element.8), kind=kLoop, calls=%fused_computation.1 | loop fusion | flops 262144 | bytes 1310720 | tf_op jit(solution)/shard_map/add | solution.py:479
